TPU v7x, 256 devices: a whole 4x4x8 slice. The times are simulated.
256 devices in a mesh: dp: 8 (over x, core), expert: 32 (over y, z).
Axes of the slice: x: 4, y: 4, z: 8, core: 2. Of those that a mesh axis runs over, the one named last changes fastest.
Arguments:
- tokens: bfloat16 [49152, 1024], P(('dp', 'expert')), may hold values from -6 to 6
- route_ids: int32 [49152, 4], P(('dp', 'expert')), may hold values from 0 to 31, all different within a row; in each aligned block of 192 rows (0 to 191, 192 to 383, ...) at most 36 rows name the same one
- gate_weight: float32 [49152, 4], P(('dp', 'expert')), may hold values from 0.25 to 1
- old_owner: int32 [32], replicated, may hold values from 0 to 31, as said below
- new_owner: int32 [32], replicated, may hold values from 0 to 31, as said below
- weights: bfloat16 [32, 3, 1024, 1024], P('expert', None, None, 'dp'), may hold values from -0.1875 to 0.1875
- first_moment: float32 [32, 3, 1024, 1024], P('expert', None, None, 'dp'), may hold values from -6 to 6
- second_moment: float32 [32, 3, 1024, 1024], P('expert', None, None, 'dp'), may hold values from 0.01 to 4
Outputs:
- layer_output: bfloat16 [49152, 1024], P(('dp', 'expert'))
- new_weights: bfloat16 [32, 3, 1024, 1024], P('expert', None, None, 'dp')
- new_first_moment: float32 [32, 3, 1024, 1024], P('expert', None, None, 'dp')
- new_second_moment: float32 [32, 3, 1024, 1024], P('expert', None, None, 'dp')
Inputs may be any that keep to these rules, and one draw needn't show every extreme that they name: `old_owner`: A permutation of the slots. `new_owner`: A permutation of the slots that differs from old_owner in exactly 5 experts. `route_ids`: the 4 experts of a row differ. In the 192 rows of one device no expert is named more than 36 times, a bound that some block reaches.
All inputs are finite; a program needn't handle non-finite values.
Results may differ from a plain program's by a relative error of at most 0.0058.
Values may be sent and summed in bfloat16 or wider, within the bound.
A program may use at most 128 MiB of HBM per device.

v0:
```python
import jax
import jax.numpy as jnp
from jax import lax
from jax.sharding import PartitionSpec as P


def relocate_weights(weights, source_slot):
    spread = lax.all_to_all(weights, "expert", split_axis=2, concat_axis=0, tiled=True)
    ordered = jnp.take(spread, source_slot, axis=0)
    return lax.all_to_all(ordered, "expert", split_axis=0, concat_axis=2, tiled=True)


def relocate_moments(first_moment, second_moment, source_slot):
    spread = (
        lax.all_to_all(first_moment, "expert", split_axis=2, concat_axis=0, tiled=True),
        lax.all_to_all(second_moment, "expert", split_axis=2, concat_axis=0, tiled=True),
    )
    ordered = (jnp.take(spread[0], source_slot, axis=0), jnp.take(spread[1], source_slot, axis=0))
    back = (
        lax.all_to_all(ordered[0], "expert", split_axis=0, concat_axis=2, tiled=True),
        lax.all_to_all(ordered[1], "expert", split_axis=0, concat_axis=2, tiled=True),
    )
    return (back[0], back[1])


def per_device(
    tokens, route_ids, gate_weight, old_owner, new_owner, weights, first_moment, second_moment
):
    peer_count = lax.axis_size("expert")
    tok_rows = tokens.shape[0]
    top_count = route_ids.shape[1]
    experts = old_owner.shape[0]
    capacity = max(2, 3 * tok_rows * top_count // (2 * experts))
    labels = jnp.arange(experts, dtype=jnp.int32)
    source_slot = jnp.sum(
        jnp.where(new_owner[None, :] == labels[:, None], old_owner[None, :], 0), axis=1
    )
    moved_first, moved_second = relocate_moments(first_moment, second_moment, source_slot)
    moved_weights = relocate_weights(weights, source_slot)
    expert_ids = route_ids.reshape(-1)
    target = jnp.sum(
        jnp.where(expert_ids[:, None] == labels[None, :], new_owner[None, :], 0), axis=1
    )
    matches = (target[:, None] == labels[None, :]).astype(jnp.int32)
    position = jnp.sum((jnp.cumsum(matches, axis=0) - 1) * matches, axis=1)
    slot_index = target * capacity + position
    slot_grid = slot_index.reshape(tok_rows, top_count)
    buffer_slots = jnp.arange(peer_count * capacity, dtype=jnp.int32)
    placement = jnp.any(slot_grid[None, :, :] == buffer_slots[:, None, None], axis=2).astype(
        jnp.bfloat16
    )
    outgoing = jnp.dot(placement, tokens, preferred_element_type=jnp.float32).astype(jnp.bfloat16)
    outgoing = outgoing.reshape(peer_count, capacity, tokens.shape[1])
    incoming = lax.all_to_all(outgoing, "expert", split_axis=0, concat_axis=0, tiled=True)
    received_rows = incoming.reshape(peer_count * capacity, tokens.shape[1])
    shard_piece = lax.all_gather(moved_weights, "dp", axis=3, tiled=True)
    gate_part = jnp.dot(received_rows, shard_piece[0, 0], preferred_element_type=jnp.float32)
    up_part = jnp.dot(received_rows, shard_piece[0, 1], preferred_element_type=jnp.float32)
    hidden = (jax.nn.silu(gate_part) * up_part).astype(jnp.bfloat16)
    accumulated = jnp.einsum(
        "rh,dh->rd", hidden, shard_piece[0, 2], preferred_element_type=jnp.float32
    )
    answers = accumulated.astype(jnp.bfloat16).reshape(peer_count, capacity, tokens.shape[1])
    returned = lax.all_to_all(answers, "expert", split_axis=0, concat_axis=0, tiled=True)
    returned = returned.reshape(peer_count * capacity, tokens.shape[1])
    picked = (
        jnp.take(returned, slot_index, axis=0)
        .astype(jnp.float32)
        .reshape(tok_rows, top_count, tokens.shape[1])
    )
    layer_output = jnp.sum(picked * gate_weight[:, :, None], axis=1).astype(jnp.bfloat16)
    return (layer_output, moved_weights, moved_first, moved_second)


def solution(mesh):
    placed = (
        P(("dp", "expert"), None),
        P(("dp", "expert"), None),
        P(("dp", "expert"), None),
        P(),
        P(),
        P("expert", None, None, "dp"),
        P("expert", None, None, "dp"),
        P("expert", None, None, "dp"),
    )
    return jax.shard_map(
        per_device,
        mesh=mesh,
        in_specs=placed,
        out_specs=(
            P(("dp", "expert"), None),
            P("expert", None, None, "dp"),
            P("expert", None, None, "dp"),
            P("expert", None, None, "dp"),
        ),
        check_vma=False,
    )
```

profile of v0, /device:TPU:2, one launch (start us, length us, event | category | flops | bytes accessed | tf_op | source)
XLA Modules:
  0.0 434.6 jit_solution(15613152316707516499)
XLA Ops:
  10.0 11.5 %all-to-all-start.1 = ((bf16[1,3,1024,128]{3,1,0,2:T(4,128)(2,1)}), bf16[1,3,1024,128]{3,1,0,2:T(4,128)(2,1)S(1)}, u32[]{:S(2)}, u32[]{:S(2)}) async-start(bf16[1,3,1024,128]{3,1,0,2:T(4,128)(2,1)} %copy.43), calls=%async_computation.1 | async-start | bytes 2097152 | tf_op jit(solution)/shard_map/all_to_all | solution.py:8
  21.7 28.5 %all-to-all-done.1 = bf16[1,3,1024,128]{3,1,0,2:T(4,128)(2,1)S(1)} async-done(((bf16[1,3,1024,128]{3,1,0,2:T(4,128)(2,1)}), bf16[1,3,1024,128]{3,1,0,2:T(4,128)(2,1)S(1)}, u32[]{:S(2)}, u32[]{:S(2)}) %all-to-all-start.1) | async-done | bytes 786464 | tf_op jit(solution)/shard_map/all_to_all | solution.py:8
  52.0 5.1 %all-to-all-start.2 = ((bf16[32,3,32,128]{3,2,1,0:T(8,128)(2,1)}), bf16[32,3,32,128]{3,2,1,0:T(8,128)(2,1)S(1)}, u32[]{:S(2)}, u32[]{:S(2)}) async-start(bf16[32,3,32,128]{3,2,1,0:T(8,128)(2,1)} %broadcast_select_fusion.2), calls=%async_computation.2 | async-start | bytes 1572864 | tf_op jit(solution)/shard_map/all_to_all | solution.py:10
  57.1 3.8 copy.48
  61.0 19.0 %all-to-all-done.2 = bf16[32,3,32,128]{3,2,1,0:T(8,128)(2,1)S(1)} async-done(((bf16[32,3,32,128]{3,2,1,0:T(8,128)(2,1)}), bf16[32,3,32,128]{3,2,1,0:T(8,128)(2,1)S(1)}, u32[]{:S(2)}, u32[]{:S(2)}) %all-to-all-start.2) | async-done | bytes 786464 | tf_op jit(solution)/shard_map/all_to_all | solution.py:10
  79.9 4.8 %all-to-all-start.4 = ((f32[1,3,1024,128]{3,1,0,2:T(4,128)}), f32[1,3,1024,128]{3,1,0,2:T(4,128)S(1)}, u32[]{:S(2)}, u32[]{:S(2)}) async-start(f32[1,3,1024,128]{3,1,0,2:T(4,128)} %copy.48), calls=%async_computation.4 | async-start | bytes 4194304 | tf_op jit(solution)/shard_map/all_to_all | solution.py:15
  84.7 3.9 copy.52
  88.6 45.7 %all-to-all-done.4 = f32[1,3,1024,128]{3,1,0,2:T(4,128)S(1)} async-done(((f32[1,3,1024,128]{3,1,0,2:T(4,128)}), f32[1,3,1024,128]{3,1,0,2:T(4,128)S(1)}, u32[]{:S(2)}, u32[]{:S(2)}) %all-to-all-start.4) | async-done | bytes 1572896 | tf_op jit(solution)/shard_map/all_to_all | solution.py:15
  134.3 6.0 %all-to-all-start.6 = ((f32[1,3,1024,128]{3,1,0,2:T(4,128)}), f32[1,3,1024,128]{3,1,0,2:T(4,128)}, u32[]{:S(2)}, u32[]{:S(2)}) async-start(f32[1,3,1024,128]{3,1,0,2:T(4,128)} %copy.52), calls=%async_computation.6 | async-start | bytes 4194304 | tf_op jit(solution)/shard_map/all_to_all | solution.py:16
  147.7 42.2 %all-to-all-done.6 = f32[1,3,1024,128]{3,1,0,2:T(4,128)} async-done(((f32[1,3,1024,128]{3,1,0,2:T(4,128)}), f32[1,3,1024,128]{3,1,0,2:T(4,128)}, u32[]{:S(2)}, u32[]{:S(2)}) %all-to-all-start.6) | async-done | bytes 1572896 | tf_op jit(solution)/shard_map/all_to_all | solution.py:16
  189.9 6.0 %all-to-all-start = ((bf16[32,36,1024]{2,1,0:T(8,128)(2,1)}), bf16[32,36,1024]{2,1,0:T(8,128)(2,1)S(1)}, u32[]{:S(2)}, u32[]{:S(2)}) async-start(bf16[32,36,1024]{2,1,0:T(8,128)(2,1)} %reshape.119), calls=%async_computation | async-start | bytes 5242880 | tf_op jit(solution)/shard_map/all_to_all | solution.py:54
  201.8 3.2 gather_fusion.2
  208.2 4.1 broadcast_select_fusion
  212.4 46.4 %all-to-all-done = bf16[32,36,1024]{2,1,0:T(8,128)(2,1)S(1)} async-done(((bf16[32,36,1024]{2,1,0:T(8,128)(2,1)}), bf16[32,36,1024]{2,1,0:T(8,128)(2,1)S(1)}, u32[]{:S(2)}, u32[]{:S(2)}) %all-to-all-start) | async-done | bytes 2359328 | tf_op jit(solution)/shard_map/all_to_all | solution.py:54
  258.8 43.9 %all_to_all.118 = f32[32,3,32,128]{3,2,1,0:T(8,128)} all-to-all(f32[32,3,32,128]{3,2,1,0:T(8,128)} %get-tuple-element.6), channel_id=1, replica_groups=mesh['dp'=8,'expert'=32] {'expert'}, dimensions={0} | all-to-all | bytes 3145728 | tf_op jit(solution)/shard_map/all_to_all | solution.py:20
  302.7 5.2 %all-to-all-start.7 = ((f32[32,3,32,128]{3,2,1,0:T(8,128)}), f32[32,3,32,128]{3,2,1,0:T(8,128)}, u32[]{:S(2)}, u32[]{:S(2)}) async-start(f32[32,3,32,128]{3,2,1,0:T(8,128)} %get-tuple-element.5), calls=%async_computation.7 | async-start | bytes 3145728 | tf_op jit(solution)/shard_map/all_to_all | solution.py:21
  310.0 7.3 %fusion.2 = f32[1152,1024]{1,0:T(8,128)} fusion(bf16[1152,1024]{1,0:T(8,128)(2,1)} %reshape.120, bf16[1,3,1024,1024]{3,2,1,0:T(8,128)(2,1)} %all-gather.2.cloned.1.call-done), kind=kOutput, calls=%fused_computation.14 | convolution fusion | flops 2415919104 | bytes 9175040 | tf_op jit(solution)/shard_map/dot_general | solution.py:57
  317.3 10.2 %convolution_convert_fusion = bf16[1152,1024]{1,0:T(8,128)(2,1)} fusion(bf16[1,3,1024,1024]{3,2,1,0:T(8,128)(2,1)} %all-gather.2.cloned.1.call-done, bf16[1152,1024]{1,0:T(8,128)(2,1)S(1)} %copy-done.4, f32[1152,1024]{1,0:T(8,128)} %fusion.2), kind=kOutput, calls=%fused_computation.5 | convolution fusion | flops 4840095744 | bytes 13631488 | tf_op jit(solution)/shard_map/rh,dh->rd/dot_general | solution.py:60
  327.5 4.1 reshape.121
  331.6 15.0 %all-to-all-done.7 = f32[32,3,32,128]{3,2,1,0:T(8,128)} async-done(((f32[32,3,32,128]{3,2,1,0:T(8,128)}), f32[32,3,32,128]{3,2,1,0:T(8,128)}, u32[]{:S(2)}, u32[]{:S(2)}) %all-to-all-start.7) | async-done | bytes 1572896 | tf_op jit(solution)/shard_map/all_to_all | solution.py:21
  346.6 5.6 %all-to-all-start.3 = ((bf16[32,36,1024]{2,1,0:T(8,128)(2,1)}), bf16[32,36,1024]{2,1,0:T(8,128)(2,1)}, u32[]{:S(2)}, u32[]{:S(2)}) async-start(bf16[32,36,1024]{2,1,0:T(8,128)(2,1)} %reshape.121), calls=%async_computation.3 | async-start | bytes 5242880 | tf_op jit(solution)/shard_map/all_to_all | solution.py:64
  356.4 58.7 %all-to-all-done.3 = bf16[32,36,1024]{2,1,0:T(8,128)(2,1)} async-done(((bf16[32,36,1024]{2,1,0:T(8,128)(2,1)}), bf16[32,36,1024]{2,1,0:T(8,128)(2,1)}, u32[]{:S(2)}, u32[]{:S(2)}) %all-to-all-start.3) | async-done | bytes 2359328 | tf_op jit(solution)/shard_map/all_to_all | solution.py:64
  417.7 3.6 gather_fusion.1
  423.8 3.9 multiply_reduce_fusion
  (58 shorter events, 32.8 us)
Async XLA Ops:
  7.2 137.5 %copy-start = (bf16[192,1024]{1,0:T(8,128)(2,1)S(1)}, bf16[192,1024]{1,0:T(8,128)(2,1)}, u32[]{:S(2)}) copy-start(bf16[192,1024]{1,0:T(8,128)(2,1)} %param.10) | copy-start | bytes 1179652
  7.2 14.3 %copy-start.7 = (s32[32]{0:T(128)S(1)}, s32[32]{0:T(128)}, u32[]{:S(2)}) copy-start(s32[32]{0:T(128)} %param.14) | copy-start | bytes 388
  7.2 14.3 %copy-start.8 = (s32[32]{0:T(128)S(1)}, s32[32]{0:T(128)}, u32[]{:S(2)}) copy-start(s32[32]{0:T(128)} %param.13) | copy-start | bytes 388
  10.0 40.1 %all-to-all-start.1 = ((bf16[1,3,1024,128]{3,1,0,2:T(4,128)(2,1)}), bf16[1,3,1024,128]{3,1,0,2:T(4,128)(2,1)S(1)}, u32[]{:S(2)}, u32[]{:S(2)}) async-start(bf16[1,3,1024,128]{3,1,0,2:T(4,128)(2,1)} %copy.43), calls=%async_computation.1 | async-start | bytes 2097152 | tf_op jit(solution)/shard_map/all_to_all | solution.py:8
  52.0 27.9 %all-to-all-start.2 = ((bf16[32,3,32,128]{3,2,1,0:T(8,128)(2,1)}), bf16[32,3,32,128]{3,2,1,0:T(8,128)(2,1)S(1)}, u32[]{:S(2)}, u32[]{:S(2)}) async-start(bf16[32,3,32,128]{3,2,1,0:T(8,128)(2,1)} %broadcast_select_fusion.2), calls=%async_computation.2 | async-start | bytes 1572864 | tf_op jit(solution)/shard_map/all_to_all | solution.py:10
  79.9 54.3 %all-to-all-start.4 = ((f32[1,3,1024,128]{3,1,0,2:T(4,128)}), f32[1,3,1024,128]{3,1,0,2:T(4,128)S(1)}, u32[]{:S(2)}, u32[]{:S(2)}) async-start(f32[1,3,1024,128]{3,1,0,2:T(4,128)} %copy.48), calls=%async_computation.4 | async-start | bytes 4194304 | tf_op jit(solution)/shard_map/all_to_all | solution.py:15
  88.6 52.7 %copy-start.5 = (s32[192,4]{0,1:T(4,128)S(1)}, s32[192,4]{0,1:T(4,128)}, u32[]{:S(2)}) copy-start(s32[192,4]{0,1:T(4,128)} %param.11) | copy-start | bytes 9220
  134.3 7.0 %copy-start.2 = (f32[1,3,1024,128]{3,1,0,2:T(4,128)}, f32[1,3,1024,128]{3,1,0,2:T(4,128)S(1)}, u32[]{:S(2)}) copy-start(f32[1,3,1024,128]{3,1,0,2:T(4,128)S(1)} %all-to-all-done.4) | copy-start | bytes 4718596
  134.3 55.6 %all-to-all-start.6 = ((f32[1,3,1024,128]{3,1,0,2:T(4,128)}), f32[1,3,1024,128]{3,1,0,2:T(4,128)}, u32[]{:S(2)}, u32[]{:S(2)}) async-start(f32[1,3,1024,128]{3,1,0,2:T(4,128)} %copy.52), calls=%async_computation.6 | async-start | bytes 4194304 | tf_op jit(solution)/shard_map/all_to_all | solution.py:16
  140.2 169.8 %all-gather.2.cloned.1.call-start = ((), (), s32[]{:S(2)}) async-start(), calls=%async_computation.8 | async-start | bytes 7077888 | tf_op jit(solution)/shard_map/all_gather | solution.py:56
  189.9 68.9 %all-to-all-start = ((bf16[32,36,1024]{2,1,0:T(8,128)(2,1)}), bf16[32,36,1024]{2,1,0:T(8,128)(2,1)S(1)}, u32[]{:S(2)}, u32[]{:S(2)}) async-start(bf16[32,36,1024]{2,1,0:T(8,128)(2,1)} %reshape.119), calls=%async_computation | async-start | bytes 5242880 | tf_op jit(solution)/shard_map/all_to_all | solution.py:54
  302.7 43.9 %all-to-all-start.7 = ((f32[32,3,32,128]{3,2,1,0:T(8,128)}), f32[32,3,32,128]{3,2,1,0:T(8,128)}, u32[]{:S(2)}, u32[]{:S(2)}) async-start(f32[32,3,32,128]{3,2,1,0:T(8,128)} %get-tuple-element.5), calls=%async_computation.7 | async-start | bytes 3145728 | tf_op jit(solution)/shard_map/all_to_all | solution.py:21
  310.0 7.3 %copy-start.4 = (bf16[1152,1024]{1,0:T(8,128)(2,1)S(1)}, bf16[1152,1024]{1,0:T(8,128)(2,1)}, u32[]{:S(2)}) copy-start(bf16[1152,1024]{1,0:T(8,128)(2,1)} %reshape.120) | copy-start | bytes 7077892
  331.6 20.6 %copy-start.6 = (f32[192,4]{0,1:T(4,128)S(1)}, f32[192,4]{0,1:T(4,128)}, u32[]{:S(2)}) copy-start(f32[192,4]{0,1:T(4,128)} %param.12) | copy-start | bytes 9220
  331.6 20.8 %copy-start.3 = (f32[32,3,32,128]{3,2,1,0:T(8,128)S(1)}, f32[32,3,32,128]{3,2,1,0:T(8,128)}, u32[]{:S(2)}) copy-start(f32[32,3,32,128]{3,2,1,0:T(8,128)} %all_to_all.118) | copy-start | bytes 4718596
  346.6 68.5 %all-to-all-start.3 = ((bf16[32,36,1024]{2,1,0:T(8,128)(2,1)}), bf16[32,36,1024]{2,1,0:T(8,128)(2,1)}, u32[]{:S(2)}, u32[]{:S(2)}) async-start(bf16[32,36,1024]{2,1,0:T(8,128)(2,1)} %reshape.121), calls=%async_computation.3 | async-start | bytes 5242880 | tf_op jit(solution)/shard_map/all_to_all | solution.py:64
  417.7 10.0 %copy-start.1 = (bf16[192,1024]{1,0:T(8,128)(2,1)S(1)}, bf16[192,1024]{1,0:T(8,128)(2,1)}, u32[]{:S(2)}) copy-start(bf16[192,1024]{1,0:T(8,128)(2,1)} %param.10) | copy-start | bytes 1179652
Sparse Core Ops, SparseCore 0:
  143.5 48.5 all-gather.1
where the time goes:
time: 436 us; the launch traced here: 435 us
  waiting for transfers between devices  255 us (58%)
  local copies, waits for them, and re-layouts  46.6 us (11%)
  starting transfers between devices  44.1 us (10%)
  blocking collectives  43.9 us (10%)
  matrix products  18.3 us (4%)
  between operations  14.3 us (3%)
  other arithmetic  11.9 us (3%)
    all_to_all x1, waiting for transfers between devices, per_device(): lax.all_to_all(answers, 'expert', split_axis=0, concat_axis=0, tiled=True)  58.7 us
    all_to_all x1, waiting for transfers between devices, per_device(): lax.all_to_all(outgoing, 'expert', split_axis=0, concat_axis=0, tiled=True)  46.4 us
    all_to_all x1, waiting for transfers between devices, relocate_moments(): lax.all_to_all(first_moment, 'expert', split_axis=2, concat_axis=0, tiled...  45.7 us
    all_to_all x1, blocking collectives, relocate_moments(): lax.all_to_all(ordered[0], 'expert', split_axis=0, concat_axis=2, tiled=T...  43.9 us
    all_to_all x1, waiting for transfers between devices, relocate_moments(): lax.all_to_all(second_moment, 'expert', split_axis=2, concat_axis=0, tile...  42.2 us
    all_to_all x1, waiting for transfers between devices, relocate_weights(): lax.all_to_all(weights, 'expert', split_axis=2, concat_axis=0, tiled=True)  28.5 us
    all_to_all x1, waiting for transfers between devices, relocate_weights(): lax.all_to_all(ordered, 'expert', split_axis=0, concat_axis=2, tiled=True)  19 us
    all_to_all x1, waiting for transfers between devices, relocate_moments(): lax.all_to_all(ordered[1], 'expert', split_axis=0, concat_axis=2, tiled=T...  15 us
  transfers between devices with their start and end apart: 8, of which 7 were waited for; matrix products, arithmetic and copies ran while one was open for 14% of the time, Pallas kernels for 0%

commit v1 on v0

--- a/solution.py
+++ b/solution.py
@@ -2,6 +2,12 @@
 import jax.numpy as jnp
 from jax import lax
 from jax.sharding import PartitionSpec as P
+
+
+def exchange_blocks(shard, axis, split, join):
+    shards = jnp.split(shard, lax.axis_size(axis), axis=split)
+    received = lax.all_to_all(jnp.stack(shards), axis, 0, 0)
+    return jnp.concatenate(received, axis=join)
 
 
 def relocate_weights(weights, source_slot):
@@ -13,7 +19,7 @@
 def relocate_moments(first_moment, second_moment, source_slot):
     spread = (
         lax.all_to_all(first_moment, "expert", split_axis=2, concat_axis=0, tiled=True),
-        lax.all_to_all(second_moment, "expert", split_axis=2, concat_axis=0, tiled=True),
+        exchange_blocks(second_moment, "expert", 2, 0),
     )
     ordered = (jnp.take(spread[0], source_slot, axis=0), jnp.take(spread[1], source_slot, axis=0))
     back = (

time: 436 us -> 426 us (0.977)
  waiting for transfers between devices: 255 us -> 226 us
  local copies, waits for them, and re-layouts: 46.6 us -> 66.6 us
    unnamed x23 -> x55, local copies, waits for them, and re-layouts: 10.8 us -> 32.3 us
    all_to_all x1, waiting for transfers between devices: 28.5 us -> 12.9 us  [relocate_weights(): lax.all_to_all(weights, 'expert', split_axis=2, concat_axis=0, tiled=True)]
    all_to_all x1, waiting for transfers between devices: 42.2 us -> 34.8 us  [exchange_blocks(): received = lax.all_to_all(jnp.stack(shards), axis, 0, 0)]
    all_to_all x1, waiting for transfers between devices: 19 us -> 12.9 us  [relocate_weights(): lax.all_to_all(ordered, 'expert', split_axis=0, concat_axis=2, tiled=True)]
  transfers between devices with their start and end apart: 8 -> 8, of which waited for: 7 -> 7; matrix products, arithmetic and copies ran while one was open for 14% -> 18% of each run, Pallas kernels for 0% -> 0%
where the time goes in v1:
time: 426 us; the launch traced here: 425 us
  waiting for transfers between devices  226 us (53%)
  local copies, waits for them, and re-layouts  66.6 us (16%)
  blocking collectives  43.9 us (10%)
  starting transfers between devices  43.7 us (10%)
  matrix products  18.3 us (4%)
  between operations  14.4 us (3%)
  other arithmetic  11.9 us (3%)
    all_to_all x1, waiting for transfers between devices, per_device(): lax.all_to_all(answers, 'expert', split_axis=0, concat_axis=0, tiled=True)  58.7 us
    all_to_all x1, waiting for transfers between devices, per_device(): lax.all_to_all(outgoing, 'expert', split_axis=0, concat_axis=0, tiled=True)  49.4 us
    all_to_all x1, blocking collectives, relocate_moments(): lax.all_to_all(ordered[0], 'expert', split_axis=0, concat_axis=2, tiled=T...  43.9 us
    all_to_all x1, waiting for transfers between devices, relocate_moments(): lax.all_to_all(first_moment, 'expert', split_axis=2, concat_axis=0, tiled...  42.1 us
    all_to_all x1, waiting for transfers between devices, exchange_blocks(): received = lax.all_to_all(jnp.stack(shards), axis, 0, 0)  34.8 us
    unnamed x55, local copies, waits for them, and re-layouts  32.3 us
    all_to_all x1, waiting for transfers between devices, relocate_moments(): lax.all_to_all(ordered[1], 'expert', split_axis=0, concat_axis=2, tiled=T...  15 us
    all_to_all x1, waiting for transfers between devices, relocate_weights(): lax.all_to_all(weights, 'expert', split_axis=2, concat_axis=0, tiled=True)  12.9 us
  transfers between devices with their start and end apart: 8, of which 7 were waited for; matrix products, arithmetic and copies ran while one was open for 18% of the time, Pallas kernels for 0%

profile of v1, /device:TPU:2, one launch (start us, length us, event | category | flops | bytes accessed | tf_op | source)
XLA Modules:
  0.0 424.6 jit_solution(14267793212994621301)
XLA Ops:
  10.1 11.5 %all-to-all-start.1 = ((bf16[1,3,1024,128]{3,1,0,2:T(4,128)(2,1)}), bf16[1,3,1024,128]{3,1,0,2:T(4,128)(2,1)S(1)}, u32[]{:S(2)}, u32[]{:S(2)}) async-start(bf16[1,3,1024,128]{3,1,0,2:T(4,128)(2,1)} %copy.41), calls=%async_computation.1 | async-start | bytes 2097152 | tf_op jit(solution)/shard_map/all_to_all | solution.py:14
  37.4 12.9 %all-to-all-done.1 = bf16[1,3,1024,128]{3,1,0,2:T(4,128)(2,1)S(1)} async-done(((bf16[1,3,1024,128]{3,1,0,2:T(4,128)(2,1)}), bf16[1,3,1024,128]{3,1,0,2:T(4,128)(2,1)S(1)}, u32[]{:S(2)}, u32[]{:S(2)}) %all-to-all-start.1) | async-done | bytes 786464 | tf_op jit(solution)/shard_map/all_to_all | solution.py:14
  52.1 5.1 %all-to-all-start.2 = ((bf16[32,3,32,128]{3,2,1,0:T(8,128)(2,1)}), bf16[32,3,32,128]{3,2,1,0:T(8,128)(2,1)S(1)}, u32[]{:S(2)}, u32[]{:S(2)}) async-start(bf16[32,3,32,128]{3,2,1,0:T(8,128)(2,1)} %broadcast_select_fusion.2), calls=%async_computation.2 | async-start | bytes 1572864 | tf_op jit(solution)/shard_map/all_to_all | solution.py:16
  67.2 12.9 %all-to-all-done.2 = bf16[32,3,32,128]{3,2,1,0:T(8,128)(2,1)S(1)} async-done(((bf16[32,3,32,128]{3,2,1,0:T(8,128)(2,1)}), bf16[32,3,32,128]{3,2,1,0:T(8,128)(2,1)S(1)}, u32[]{:S(2)}, u32[]{:S(2)}) %all-to-all-start.2) | async-done | bytes 786464 | tf_op jit(solution)/shard_map/all_to_all | solution.py:16
  80.0 4.8 %all-to-all-start.6 = ((f32[32,1,3,32,128]{4,3,2,1,0:T(8,128)}), f32[32,1,3,32,128]{4,3,2,1,0:T(8,128)S(1)}, u32[]{:S(2)}, u32[]{:S(2)}) async-start(f32[32,1,3,32,128]{4,3,2,1,0:T(8,128)} %constant_dynamic-update-slice_fusion), calls=%async_computation.6 | async-start | bytes 3145728 | tf_op jit(solution)/shard_map/all_to_all | solution.py:9
  84.8 3.8 copy.46
  88.7 34.8 %all-to-all-done.6 = f32[32,1,3,32,128]{4,3,2,1,0:T(8,128)S(1)} async-done(((f32[32,1,3,32,128]{4,3,2,1,0:T(8,128)}), f32[32,1,3,32,128]{4,3,2,1,0:T(8,128)S(1)}, u32[]{:S(2)}, u32[]{:S(2)}) %all-to-all-start.6) | async-done | bytes 1572896 | tf_op jit(solution)/shard_map/all_to_all | solution.py:9
  124.6 5.6 %all-to-all-start.4 = ((f32[1,3,1024,128]{3,1,0,2:T(4,128)}), f32[1,3,1024,128]{3,1,0,2:T(4,128)}, u32[]{:S(2)}, u32[]{:S(2)}) async-start(f32[1,3,1024,128]{3,1,0,2:T(4,128)} %copy.46), calls=%async_computation.4 | async-start | bytes 4194304 | tf_op jit(solution)/shard_map/all_to_all | solution.py:21
  137.7 42.1 %all-to-all-done.4 = f32[1,3,1024,128]{3,1,0,2:T(4,128)} async-done(((f32[1,3,1024,128]{3,1,0,2:T(4,128)}), f32[1,3,1024,128]{3,1,0,2:T(4,128)}, u32[]{:S(2)}, u32[]{:S(2)}) %all-to-all-start.4) | async-done | bytes 1572896 | tf_op jit(solution)/shard_map/all_to_all | solution.py:21
  179.9 6.0 %all-to-all-start = ((bf16[32,36,1024]{2,1,0:T(8,128)(2,1)}), bf16[32,36,1024]{2,1,0:T(8,128)(2,1)S(1)}, u32[]{:S(2)}, u32[]{:S(2)}) async-start(bf16[32,36,1024]{2,1,0:T(8,128)(2,1)} %reshape.122), calls=%async_computation | async-start | bytes 5242880 | tf_op jit(solution)/shard_map/all_to_all | solution.py:60
  188.9 3.2 gather_fusion.3
  192.1 3.2 gather_fusion.2
  195.3 4.1 broadcast_select_fusion
  199.4 49.4 %all-to-all-done = bf16[32,36,1024]{2,1,0:T(8,128)(2,1)S(1)} async-done(((bf16[32,36,1024]{2,1,0:T(8,128)(2,1)}), bf16[32,36,1024]{2,1,0:T(8,128)(2,1)S(1)}, u32[]{:S(2)}, u32[]{:S(2)}) %all-to-all-start) | async-done | bytes 2359328 | tf_op jit(solution)/shard_map/all_to_all | solution.py:60
  248.8 43.9 %all_to_all.105 = f32[32,3,32,128]{3,2,1,0:T(8,128)} all-to-all(f32[32,3,32,128]{3,2,1,0:T(8,128)} %get-tuple-element.6), channel_id=1, replica_groups=mesh['dp'=8,'expert'=32] {'expert'}, dimensions={0} | all-to-all | bytes 3145728 | tf_op jit(solution)/shard_map/all_to_all | solution.py:26
  292.7 5.2 %all-to-all-start.7 = ((f32[32,3,32,128]{3,2,1,0:T(8,128)}), f32[32,3,32,128]{3,2,1,0:T(8,128)}, u32[]{:S(2)}, u32[]{:S(2)}) async-start(f32[32,3,32,128]{3,2,1,0:T(8,128)} %get-tuple-element.5), calls=%async_computation.7 | async-start | bytes 3145728 | tf_op jit(solution)/shard_map/all_to_all | solution.py:27
  300.0 7.3 %fusion.2 = f32[1152,1024]{1,0:T(8,128)} fusion(bf16[1152,1024]{1,0:T(8,128)(2,1)} %reshape.123, bf16[1,3,1024,1024]{3,2,1,0:T(8,128)(2,1)} %all-gather.2.cloned.1.call-done), kind=kOutput, calls=%fused_computation.14 | convolution fusion | flops 2415919104 | bytes 9175040 | tf_op jit(solution)/shard_map/dot_general | solution.py:63
  307.3 10.2 %convolution_convert_fusion = bf16[1152,1024]{1,0:T(8,128)(2,1)} fusion(bf16[1,3,1024,1024]{3,2,1,0:T(8,128)(2,1)} %all-gather.2.cloned.1.call-done, bf16[1152,1024]{1,0:T(8,128)(2,1)S(1)} %copy-done.4, f32[1152,1024]{1,0:T(8,128)} %fusion.2), kind=kOutput, calls=%fused_computation.5 | convolution fusion | flops 4840095744 | bytes 13631488 | tf_op jit(solution)/shard_map/rh,dh->rd/dot_general | solution.py:66
  317.5 4.1 reshape.124
  321.5 15.0 %all-to-all-done.7 = f32[32,3,32,128]{3,2,1,0:T(8,128)} async-done(((f32[32,3,32,128]{3,2,1,0:T(8,128)}), f32[32,3,32,128]{3,2,1,0:T(8,128)}, u32[]{:S(2)}, u32[]{:S(2)}) %all-to-all-start.7) | async-done | bytes 1572896 | tf_op jit(solution)/shard_map/all_to_all | solution.py:27
  336.6 5.6 %all-to-all-start.3 = ((bf16[32,36,1024]{2,1,0:T(8,128)(2,1)}), bf16[32,36,1024]{2,1,0:T(8,128)(2,1)}, u32[]{:S(2)}, u32[]{:S(2)}) async-start(bf16[32,36,1024]{2,1,0:T(8,128)(2,1)} %reshape.124), calls=%async_computation.3 | async-start | bytes 5242880 | tf_op jit(solution)/shard_map/all_to_all | solution.py:70
  346.4 58.7 %all-to-all-done.3 = bf16[32,36,1024]{2,1,0:T(8,128)(2,1)} async-done(((bf16[32,36,1024]{2,1,0:T(8,128)(2,1)}), bf16[32,36,1024]{2,1,0:T(8,128)(2,1)}, u32[]{:S(2)}, u32[]{:S(2)}) %all-to-all-start.3) | async-done | bytes 2359328 | tf_op jit(solution)/shard_map/all_to_all | solution.py:70
  407.7 3.6 gather_fusion.1
  413.8 3.9 multiply_reduce_fusion
  (90 shorter events, 53.5 us)
Async XLA Ops:
  7.2 127.5 %copy-start = (bf16[192,1024]{1,0:T(8,128)(2,1)S(1)}, bf16[192,1024]{1,0:T(8,128)(2,1)}, u32[]{:S(2)}) copy-start(bf16[192,1024]{1,0:T(8,128)(2,1)} %param.10) | copy-start | bytes 1179652
  7.2 14.4 %copy-start.8 = (s32[32]{0:T(128)S(1)}, s32[32]{0:T(128)}, u32[]{:S(2)}) copy-start(s32[32]{0:T(128)} %param.14) | copy-start | bytes 388
  7.2 14.4 %copy-start.9 = (s32[32]{0:T(128)S(1)}, s32[32]{0:T(128)}, u32[]{:S(2)}) copy-start(s32[32]{0:T(128)} %param.13) | copy-start | bytes 388
  7.2 14.6 %copy-start.5 = (f32[1,3,1024,128]{3,2,1,0:T(8,128)S(1)}, f32[1,3,1024,128]{3,2,1,0:T(8,128)}, u32[]{:S(2)}) copy-start(f32[1,3,1024,128]{3,2,1,0:T(8,128)} %param.17) | copy-start | bytes 4718596
  10.1 40.1 %all-to-all-start.1 = ((bf16[1,3,1024,128]{3,1,0,2:T(4,128)(2,1)}), bf16[1,3,1024,128]{3,1,0,2:T(4,128)(2,1)S(1)}, u32[]{:S(2)}, u32[]{:S(2)}) async-start(bf16[1,3,1024,128]{3,1,0,2:T(4,128)(2,1)} %copy.41), calls=%async_computation.1 | async-start | bytes 2097152 | tf_op jit(solution)/shard_map/all_to_all | solution.py:14
  52.1 27.9 %all-to-all-start.2 = ((bf16[32,3,32,128]{3,2,1,0:T(8,128)(2,1)}), bf16[32,3,32,128]{3,2,1,0:T(8,128)(2,1)S(1)}, u32[]{:S(2)}, u32[]{:S(2)}) async-start(bf16[32,3,32,128]{3,2,1,0:T(8,128)(2,1)} %broadcast_select_fusion.2), calls=%async_computation.2 | async-start | bytes 1572864 | tf_op jit(solution)/shard_map/all_to_all | solution.py:16
  80.0 43.4 %all-to-all-start.6 = ((f32[32,1,3,32,128]{4,3,2,1,0:T(8,128)}), f32[32,1,3,32,128]{4,3,2,1,0:T(8,128)S(1)}, u32[]{:S(2)}, u32[]{:S(2)}) async-start(f32[32,1,3,32,128]{4,3,2,1,0:T(8,128)} %constant_dynamic-update-slice_fusion), calls=%async_computation.6 | async-start | bytes 3145728 | tf_op jit(solution)/shard_map/all_to_all | solution.py:9
  123.5 1.1 copy-start.3
  124.6 55.3 %all-to-all-start.4 = ((f32[1,3,1024,128]{3,1,0,2:T(4,128)}), f32[1,3,1024,128]{3,1,0,2:T(4,128)}, u32[]{:S(2)}, u32[]{:S(2)}) async-start(f32[1,3,1024,128]{3,1,0,2:T(4,128)} %copy.46), calls=%async_computation.4 | async-start | bytes 4194304 | tf_op jit(solution)/shard_map/all_to_all | solution.py:21
  130.2 1.0 copy-start.6
  130.3 169.7 %all-gather.2.cloned.1.call-start = ((), (), s32[]{:S(2)}) async-start(), calls=%async_computation.8 | async-start | bytes 7077888 | tf_op jit(solution)/shard_map/all_gather | solution.py:62
  179.9 68.9 %all-to-all-start = ((bf16[32,36,1024]{2,1,0:T(8,128)(2,1)}), bf16[32,36,1024]{2,1,0:T(8,128)(2,1)S(1)}, u32[]{:S(2)}, u32[]{:S(2)}) async-start(bf16[32,36,1024]{2,1,0:T(8,128)(2,1)} %reshape.122), calls=%async_computation | async-start | bytes 5242880 | tf_op jit(solution)/shard_map/all_to_all | solution.py:60
  292.7 43.9 %all-to-all-start.7 = ((f32[32,3,32,128]{3,2,1,0:T(8,128)}), f32[32,3,32,128]{3,2,1,0:T(8,128)}, u32[]{:S(2)}, u32[]{:S(2)}) async-start(f32[32,3,32,128]{3,2,1,0:T(8,128)} %get-tuple-element.5), calls=%async_computation.7 | async-start | bytes 3145728 | tf_op jit(solution)/shard_map/all_to_all | solution.py:27
  300.0 7.3 %copy-start.4 = (bf16[1152,1024]{1,0:T(8,128)(2,1)S(1)}, bf16[1152,1024]{1,0:T(8,128)(2,1)}, u32[]{:S(2)}) copy-start(bf16[1152,1024]{1,0:T(8,128)(2,1)} %reshape.123) | copy-start | bytes 7077892
  321.5 20.6 %copy-start.7 = (f32[192,4]{0,1:T(4,128)S(1)}, f32[192,4]{0,1:T(4,128)}, u32[]{:S(2)}) copy-start(f32[192,4]{0,1:T(4,128)} %param.12) | copy-start | bytes 9220
  321.5 20.9 %copy-start.2 = (f32[32,3,32,128]{3,2,1,0:T(8,128)S(1)}, f32[32,3,32,128]{3,2,1,0:T(8,128)}, u32[]{:S(2)}) copy-start(f32[32,3,32,128]{3,2,1,0:T(8,128)} %all_to_all.105) | copy-start | bytes 4718596
  336.6 68.5 %all-to-all-start.3 = ((bf16[32,36,1024]{2,1,0:T(8,128)(2,1)}), bf16[32,36,1024]{2,1,0:T(8,128)(2,1)}, u32[]{:S(2)}, u32[]{:S(2)}) async-start(bf16[32,36,1024]{2,1,0:T(8,128)(2,1)} %reshape.124), calls=%async_computation.3 | async-start | bytes 5242880 | tf_op jit(solution)/shard_map/all_to_all | solution.py:70
  411.3 6.5 %copy-start.1 = (bf16[192,1024]{1,0:T(8,128)(2,1)S(1)}, bf16[192,1024]{1,0:T(8,128)(2,1)}, u32[]{:S(2)}) copy-start(bf16[192,1024]{1,0:T(8,128)(2,1)} %param.10) | copy-start | bytes 1179652
Sparse Core Ops, SparseCore 0:
  133.5 48.5 all-gather.1
